TPU v7x, 32 devices: a whole 2x2x4 slice. The times are simulated.
32 devices in a mesh: section: 4 (over x, core), patch: 4 (over z), tensor: 2 (over y).
Axes of the slice: x: 2, y: 2, z: 4, core: 2. Of those that a mesh axis runs over, the one named last changes fastest.
Arguments:
- forward_input: bfloat16 [4, 1024, 1024], P('section', 'patch', 'tensor'), may hold values from -6 to 6
- backward_input: bfloat16 [4, 1024, 1024], P('section', 'patch', 'tensor'), may hold values from -6 to 6
- cotangent: bfloat16 [4, 1024, 1024], P('section', 'patch', 'tensor'), may hold values from -6 to 6
- norm_gain: float32 [4, 1024], P('section'), may hold values from 0.1 to 1.9
- projection: bfloat16 [4, 3, 1024, 1024], P('section', None, None, 'tensor'), may hold values from -6 to 6
- output_weight: bfloat16 [4, 1024, 1024], P('section', 'tensor'), may hold values from -0.1875 to 0.1875
- neighbours: int32 [1024, 9], P('patch'), may hold values from 0 to 1023, as said below
Outputs:
- forward_output: bfloat16 [4, 1024, 1024], P('section', 'patch', 'tensor')
- backward_output: bfloat16 [4, 1024, 1024], P('section', 'patch', 'tensor')
- grad_projection: float32 [4, 3, 1024, 1024], P('section', None, 'patch', 'tensor')
- grad_output_weight: float32 [4, 1024, 1024], P('section', 'tensor', 'patch')
- grad_gain: float32 [4, 1024], P('section', 'tensor')
Inputs may be any that keep to these rules, and one draw needn't show every extreme that they name: `neighbours`: row i lists 9 different pixels: i itself, and pixels whose index differs from i by at most 64 modulo 1024.
All inputs are finite; a program needn't handle non-finite values.
Results may differ from a plain program's by a relative error of at most 0.0091.
Values may be sent and summed in bfloat16 or wider, within the bound.
A program may use at most 128 MiB of HBM per device.

v0:
```python
import jax
import jax.numpy as jnp
from jax import lax
from jax.sharding import PartitionSpec as P

HEAD = 64
HALO = 64


EPSILON = 1e-06


def padded(value, sides, width):
    for axis, dim in sides:
        count, length = (lax.axis_size(axis), value.shape[dim])
        up = [(i, (i + 1) % count) for i in range(count)]
        down = [(j, i) for i, j in up]
        last = lax.slice_in_dim(value, length - width, length, axis=dim)
        first = lax.slice_in_dim(value, 0, width, axis=dim)
        before = lax.ppermute(last, axis, up)
        after = lax.ppermute(first, axis, down)
        value = jnp.concatenate([before, value, after], axis=dim)
    return value


def from_behind(value, axis, steps):
    count = lax.axis_size(axis)
    pairs = [(source, (source + steps) % count) for source in range(count)]
    return lax.ppermute(value, axis, pairs)


def prepare(inputs, gain, weights_in):
    widened = inputs.astype(jnp.float32)
    inverse = lax.rsqrt(jnp.mean(widened * widened, axis=-1, keepdims=True) + EPSILON)
    unit_rows = widened * inverse
    normed = (unit_rows * gain).astype(jnp.bfloat16)
    streams = jnp.einsum(
        "pd,cde->cpe", normed, weights_in, preferred_element_type=jnp.float32
    ).astype(jnp.bfloat16)
    return (inverse, unit_rows, normed, streams)


def spread(streams):
    return padded(streams[1:], (("patch", 1),), HALO)


def banded(rows):
    tiles = rows.shape[0] // HALO - 2
    blocks = rows.reshape(tiles + 2, HALO, rows.shape[1])
    return jnp.stack([blocks[:-2], blocks[1:-1], blocks[2:]], axis=1).reshape(
        tiles, 3 * HALO, rows.shape[1]
    )


def unband(grads):
    tiles = grads.shape[0]
    width = grads.shape[2]
    parts = grads.reshape(tiles, 3, HALO, width)
    summed = jnp.pad(parts[:, 0], ((0, 2), (0, 0), (0, 0)))
    summed = summed + jnp.pad(parts[:, 1], ((1, 1), (0, 0), (0, 0)))
    summed = summed + jnp.pad(parts[:, 2], ((2, 0), (0, 0), (0, 0)))
    return summed.reshape((tiles + 2) * HALO, width)


def attend(queries, spread_rows, allowed):
    row_count = queries.shape[0]
    tiles = row_count // HALO
    local_heads = queries.shape[1] // HEAD
    query_heads = queries.reshape(tiles, HALO, local_heads, HEAD)
    key_heads = banded(spread_rows[0]).reshape(tiles, 3 * HALO, local_heads, HEAD)
    value_heads = banded(spread_rows[1]).reshape(tiles, 3 * HALO, local_heads, HEAD)
    scores = jnp.einsum(
        "tphe,tqhe->thpq", query_heads, key_heads, preferred_element_type=jnp.float32
    ) * HEAD ** (-0.5)
    scores = jnp.where(allowed[:, None], scores, -1e30)
    maximum = jnp.max(scores, axis=-1, keepdims=True)
    exponent = jnp.exp(scores - maximum)
    weights = exponent / jnp.sum(exponent, axis=-1, keepdims=True)
    rounded = weights.astype(jnp.bfloat16)
    attended = jnp.einsum(
        "thpq,tqhe->tphe", rounded, value_heads, preferred_element_type=jnp.float32
    )
    attended = attended.astype(jnp.bfloat16).reshape(row_count, local_heads * HEAD)
    return (query_heads, key_heads, value_heads, weights, rounded, attended)


def shards(
    forward_input, backward_input, cotangent, norm_gain, projection, output_weight, neighbours
):
    row_count = neighbours.shape[0]
    tiles = row_count // HALO
    total = row_count * lax.axis_size("patch")
    half = forward_input.shape[2]
    local_heads = half // HEAD
    offset = lax.axis_index("tensor") * half
    gain = norm_gain[0]
    weights_in = projection[0]
    weights_out = output_weight[0]
    forward_whole, backward_whole, upstream = (
        lax.all_gather(forward_input[0], "tensor", axis=1, tiled=True),
        lax.all_gather(backward_input[0], "tensor", axis=1, tiled=True),
        lax.all_gather(cotangent[0], "tensor", axis=1, tiled=True),
    )
    first_row = lax.axis_index("patch") * row_count - HALO
    local_index = jnp.mod(neighbours - first_row, total)
    tile_start = jnp.arange(row_count, dtype=jnp.int32) // HALO * HALO
    relative = local_index - tile_start[:, None]
    allowed = jnp.any(
        relative[:, :, None] == jnp.arange(3 * HALO, dtype=jnp.int32)[None, None, :], axis=1
    )
    allowed = allowed.reshape(tiles, HALO, 3 * HALO)
    forward_parts = prepare(forward_whole, gain, weights_in)
    forward_streams = forward_parts[3]
    forward_spread = spread(forward_streams)
    forward_attended = attend(forward_streams[0], forward_spread, allowed)[5]
    partial_update = jnp.dot(forward_attended, weights_out, preferred_element_type=jnp.float32)
    update = lax.psum_scatter(partial_update, "tensor", scatter_dimension=1, tiled=True)
    forward_rows = (forward_input[0].astype(jnp.float32) + update).astype(jnp.bfloat16)
    inverse, unit_rows, normed, backward_streams = prepare(backward_whole, gain, weights_in)
    backward_spread = spread(backward_streams)
    query_heads, key_heads, value_heads, weights, rounded, attended = attend(
        backward_streams[0], backward_spread, allowed
    )
    grad_attended = lax.dot_general(
        upstream, weights_out, (((1,), (1,)), ((), ())), preferred_element_type=jnp.float32
    ).astype(jnp.bfloat16)
    grad_output = lax.dot_general(
        attended, upstream, (((0,), (0,)), ((), ())), preferred_element_type=jnp.float32
    )
    grad_heads = grad_attended.reshape(tiles, HALO, local_heads, HEAD)
    grad_weights = jnp.einsum(
        "tphe,tqhe->thpq", grad_heads, value_heads, preferred_element_type=jnp.float32
    )
    grad_scores = weights * (grad_weights - jnp.sum(weights * grad_weights, axis=-1, keepdims=True))
    grad_scores = (grad_scores * HEAD ** (-0.5)).astype(jnp.bfloat16)
    query_grad = jnp.einsum(
        "thpq,tqhe->tphe", grad_scores, key_heads, preferred_element_type=jnp.float32
    ).reshape(row_count, half)
    key_band = jnp.einsum(
        "thpq,tphe->tqhe", grad_scores, query_heads, preferred_element_type=jnp.float32
    )
    value_band = jnp.einsum(
        "thpq,tphe->tqhe", rounded, grad_heads, preferred_element_type=jnp.float32
    )
    key_grad = unband(key_band.reshape(tiles, 3 * HALO, half))
    value_grad = unband(value_band.reshape(tiles, 3 * HALO, half))
    spread_grad = jnp.stack([key_grad, value_grad])
    rim_rows = jnp.concatenate([spread_grad[:, :HALO], spread_grad[:, row_count + HALO :]], axis=1)
    returned = padded(rim_rows, (("patch", 1),), HALO)
    middle = spread_grad[:, HALO : HALO + row_count]
    owned = jnp.concatenate(
        [
            middle[:, :HALO] + returned[:, :HALO],
            middle[:, HALO : row_count - HALO],
            middle[:, row_count - HALO :] + returned[:, 3 * HALO :],
        ],
        axis=1,
    )
    stream_grads = jnp.concatenate([query_grad[None], owned], axis=0).astype(jnp.bfloat16)
    grad_normed = jnp.einsum(
        "cpe,cde->pd", stream_grads, weights_in, preferred_element_type=jnp.float32
    )
    grad_weights_in = jnp.einsum(
        "pd,cpe->cde", normed, stream_grads, preferred_element_type=jnp.float32
    )
    projection_share, output_share = (
        lax.psum_scatter(grad_weights_in, "patch", scatter_dimension=1, tiled=True),
        lax.psum_scatter(grad_output, "patch", scatter_dimension=1, tiled=True),
    )
    grad_whole = lax.psum(grad_normed, "tensor")
    scaled = grad_whole * gain
    correction = jnp.mean(scaled * unit_rows, axis=-1, keepdims=True)
    grad_full = inverse * (scaled - unit_rows * correction)
    grad_local = lax.dynamic_slice_in_dim(grad_full, offset, half, 1)
    gain_local = lax.dynamic_slice_in_dim(jnp.sum(grad_whole * unit_rows, axis=0), offset, half, 0)
    gain_share = lax.psum(gain_local, "patch")
    backward_rows = (cotangent[0].astype(jnp.float32) + grad_local).astype(jnp.bfloat16)
    forward_sent = from_behind(forward_rows, "section", 1)
    backward_sent = from_behind(backward_rows, "section", -1)
    return (
        forward_sent[None],
        backward_sent[None],
        projection_share[None],
        output_share[None],
        gain_share[None],
    )


def solution(mesh):
    return jax.shard_map(
        shards,
        mesh=mesh,
        in_specs=(
            P("section", "patch", "tensor"),
            P("section", "patch", "tensor"),
            P("section", "patch", "tensor"),
            P("section", None),
            P("section", None, None, "tensor"),
            P("section", "tensor", None),
            P("patch", None),
        ),
        out_specs=(
            P("section", "patch", "tensor"),
            P("section", "patch", "tensor"),
            P("section", None, "patch", "tensor"),
            P("section", "tensor", "patch"),
            P("section", "tensor"),
        ),
        check_vma=False,
    )
```

profile of v0, /device:TPU:0, one launch (start us, length us, event | category | flops | bytes accessed | tf_op | source)
XLA Modules:
  0.0 396.3 jit_solution(8001144368191026523)
XLA Ops:
  7.2 10.3 %all-gather = bf16[1,256,1024]{2,1,0:T(8,128)(2,1)S(1)} all-gather(bf16[1,256,512]{2,1,0:T(8,128)(2,1)} %param.7), channel_id=2, replica_groups=mesh['section'=4,'patch'=4,'tensor'=2] {'tensor'}, dimensions={2}, use_global_device_ids=true | all-gather | bytes 786432 | tf_op jit(solution)/shard_map/all_gather | solution.py:100
  24.2 7.6 %all-gather.1 = bf16[1,256,1024]{2,1,0:T(8,128)(2,1)S(1)} all-gather(bf16[1,256,512]{2,1,0:T(8,128)(2,1)S(1)} %copy-done.17), channel_id=3, replica_groups=mesh['section'=4,'patch'=4,'tensor'=2] {'tensor'}, dimensions={2}, use_global_device_ids=true | all-gather | bytes 786432 | tf_op jit(solution)/shard_map/all_gather | solution.py:101
  33.8 3.8 collective-permute-start.4
  39.8 7.2 %all-gather.2 = bf16[1,256,1024]{2,1,0:T(8,128)(2,1)S(1)} all-gather(bf16[1,256,512]{2,1,0:T(8,128)(2,1)S(1)} %copy-done.13), channel_id=4, replica_groups=mesh['section'=4,'patch'=4,'tensor'=2] {'tensor'}, dimensions={2}, use_global_device_ids=true | all-gather | bytes 786432 | tf_op jit(solution)/shard_map/all_gather | solution.py:102
  63.9 3.2 reshape_reshape.20
  67.1 2.7 copy.121
  71.8 3.2 reshape_reshape.21
  75.0 2.7 copy.120
  77.8 3.2 fusion.132
  81.0 3.6 fusion.131
  84.5 3.6 convolution_bitcast_fusion.1
  88.2 16.2 %convolution_bitcast_fusion.2 = f32[4,192,8,64]{1,3,2,0:T(8,128)} fusion(bf16[4,64,8,64]{1,3,2,0:T(8,128)(2,1)} %copy.123, f32[4,8,64,192]{3,2,1,0:T(8,128)} %fusion.132, f32[4,8,64,192]{3,2,1,0:T(8,128)} %get-tuple-element.60, f32[4,8,64]{2,1,0:T(8,128)S(1)} %get-tuple-element.59), kind=kOutput, calls=%fused_computation.31 | convolution fusion | flops 53086400 | bytes 4988928 | tf_op jit(solution)/shard_map/thpq,tphe->tqhe/dot_general | solution.py:139
  104.4 3.4 copy.128
  107.8 3.7 reshape_reshape.23
  114.1 3.4 copy.124
  117.5 3.7 reshape_reshape.22
  127.4 3.2 reshape_reshape.19
  132.6 3.2 reshape_reshape.18
  137.7 3.4 collective-permute-start.6
  141.1 15.8 %fusion.46 = bf16[4,64,8,64]{1,3,2,0:T(8,128)(2,1)} fusion(bf16[4,192,8,64]{1,3,2,0:T(8,128)(2,1)} %copy.121, f32[4,8,64,192]{3,2,1,0:T(8,128)} %fusion.132, f32[4,8,64,192]{3,2,1,0:T(8,128)} %get-tuple-element.60, f32[4,8,64]{2,1,0:T(8,128)S(1)} %copy-done.22), kind=kOutput, calls=%fused_computation.50 | convolution fusion | flops 53217472 | bytes 4202496 | tf_op jit(solution)/shard_map/thpq,tqhe->tphe/dot_general | solution.py:136
  165.6 3.4 fusion.126
  169.0 4.1 %fusion.22 = f32[4,8,64,192]{3,2,1,0:T(8,128)} fusion(bf16[4,192,8,64]{3,2,1,0:T(8,128)(2,1)} %reshape_reshape.19, bf16[4,64,8,64]{3,2,1,0:T(8,128)(2,1)} %reshape_squeeze.4), kind=kOutput, calls=%fused_computation.35 | convolution fusion | flops 50331648 | bytes 2621440 | tf_op jit(solution)/shard_map/tphe,tqhe->thpq/dot_general | solution.py:72
  173.1 7.0 %fusion.49 = bf16[4,64,8,64]{1,3,2,0:T(8,128)(2,1)} fusion(bf16[4,192,8,64]{3,2,1,0:T(8,128)(2,1)} %reshape_reshape.18, f32[4,8,64]{2,1,0:T(8,128)} %fusion.126, f32[4,8,64,192]{3,2,1,0:T(8,128)} %fusion.22, pred[4,64,192]{2,1,0:T(8,128)(4,1)} %bitcast.191), kind=kOutput, calls=%fused_computation.51 | convolution fusion | flops 52431040 | bytes 2678784 | tf_op jit(solution)/shard_map/thpq,tqhe->tphe/dot_general | solution.py:80
  184.3 2.7 fusion.57
  187.1 5.0 %convolution_bitcast_fusion = f32[3,1024,512]{1,2,0:T(8,128)} fusion(bf16[2,64,512]{2,1,0:T(8,128)(2,1)} %copy-done.16, bf16[2,128,512]{2,1,0:T(8,128)(2,1)} %copy-done.12, bf16[2,64,512]{2,1,0:T(8,128)(2,1)S(1)} %get-tuple-element.28, bf16[1,256,512]{2,1,0:T(8,128)(2,1)S(1)} %broadcast_in_dim_reshape.6, bf16[1,256,1024]{2,1,0:T(8,128)(2,1)} %copy-done.5, ...), kind=kOutput, calls=%fused_computation.9 | convolution fusion | flops 809500672 | bytes 7607296 | tf_op jit(solution)/shard_map/pd,cpe->cde/dot_general | solution.py:163
  192.8 3.2 fusion.45
  199.5 2.8 fusion.76
  207.5 19.6 %reduce-scatter.4.cloned.1.call-done = f32[256,512]{1,0:T(8,128)} async-done(((f32[256,1024]{1,0:T(8,128)}), f32[256,512]{1,0:T(8,128)}) %reduce-scatter.4.cloned.1.call-update) | async-done | bytes 524304 | tf_op jit(solution)/shard_map/reduce_scatter | solution.py:117
  229.1 12.3 %psum.15 = f32[1,512]{1,0:T(1,128)} all-reduce(f32[1,512]{1,0:T(1,128)S(1)} %bitcast.196), channel_id=1, replica_groups=mesh['section'=4,'patch'=4,'tensor'=2] {'patch'}, use_global_device_ids=true, to_apply=%region_14.15 | all-reduce | flops 512 | bytes 4096 | tf_op jit(solution)/shard_map/psum | solution.py:176
  241.5 98.9 %reduce-scatter.6.cloned.1.call-done = f32[3,256,512]{1,2,0:T(8,128)} async-done(((f32[3,1024,512]{1,2,0:T(8,128)}), f32[3,256,512]{1,2,0:T(8,128)}) %reduce-scatter.6.cloned.1.call-update) | async-done | bytes 1572880 | tf_op jit(solution)/shard_map/reduce_scatter | solution.py:167
  340.3 3.0 copy.134
  343.4 44.1 %reduce-scatter.8.cloned.1.call-done = f32[512,256]{1,0:T(8,128)} async-done(((f32[512,1024]{1,0:T(8,128)}), f32[512,256]{1,0:T(8,128)}) %reduce-scatter.8.cloned.1.call-update) | async-done | bytes 524304 | tf_op jit(solution)/shard_map/reduce_scatter | solution.py:168
  (122 shorter events, 68.7 us)
Async XLA Ops:
  7.2 10.5 %copy-start = (bf16[1,3,1024,512]{3,2,1,0:T(8,128)(2,1)S(1)}, bf16[1,3,1024,512]{3,2,1,0:T(8,128)(2,1)}, u32[]{:S(2)}) copy-start(bf16[1,3,1024,512]{3,2,1,0:T(8,128)(2,1)} %param.11) | copy-start | bytes 9437188
  7.2 196.7 %all-reduce.8.cloned.1.call-start = ((), (), s32[]{:S(2)}) async-start(), calls=%async_computation.4 | async-start | bytes 2097152 | tf_op jit(solution)/shard_map/psum | solution.py:170
  17.7 6.5 %copy-start.17 = (bf16[1,256,512]{2,1,0:T(8,128)(2,1)S(1)}, bf16[1,256,512]{2,1,0:T(8,128)(2,1)}, u32[]{:S(2)}) copy-start(bf16[1,256,512]{2,1,0:T(8,128)(2,1)} %param.8) | copy-start | bytes 786436
  17.7 14.2 %copy-start.19 = (f32[1,1024]{1,0:T(1,128)S(1)}, f32[1,1024]{1,0:T(1,128)}, u32[]{:S(2)}) copy-start(f32[1,1024]{1,0:T(1,128)} %param.10) | copy-start | bytes 12292
  19.6 18.1 %copy-start.8 = (bf16[3,256,512]{2,1,0:T(8,128)(2,1)}, bf16[3,256,512]{2,1,0:T(8,128)(2,1)S(1)}, u32[]{:S(2)}) copy-start(bf16[3,256,512]{2,1,0:T(8,128)(2,1)S(1)} %fusion.36) | copy-start | bytes 2359300
  20.4 104.2 %collective-permute-start = (bf16[2,64,512]{2,1,0:T(8,128)(2,1)}, bf16[2,64,512]{2,1,0:T(8,128)(2,1)}, u32[]{:S(2)}, u32[]{:S(2)}) collective-permute-start(bf16[2,64,512]{2,1,0:T(8,128)(2,1)} %get-tuple-element.44), channel_id=1, source_target_pairs={{0,2},{2,4},{4,6},{6,0},{1,3},{3,5},{5,7},{7,1},{8,10},{10,12},{12... | collective-permute-start | bytes 393224 | tf_op jit(solution)/shard_map/ppermute | solution.py:20
  22.2 102.4 %collective-permute-start.1 = (bf16[2,64,512]{2,1,0:T(8,128)(2,1)}, bf16[2,64,512]{2,1,0:T(8,128)(2,1)}, u32[]{:S(2)}, u32[]{:S(2)}) collective-permute-start(bf16[2,64,512]{2,1,0:T(8,128)(2,1)} %get-tuple-element.45), channel_id=1, source_target_pairs={{2,0},{4,2},{6,4},{0,6},{3,1},{5,3},{7,5},{1,7},{10,8},{12,10},{14... | collective-permute-start | bytes 393224 | tf_op jit(solution)/shard_map/ppermute | solution.py:21
  31.8 1.3 copy-start.5
  33.1 5.5 %copy-start.7 = (bf16[3,256,512]{2,1,0:T(8,128)(2,1)}, bf16[3,256,512]{2,1,0:T(8,128)(2,1)S(1)}, u32[]{:S(2)}) copy-start(bf16[3,256,512]{2,1,0:T(8,128)(2,1)S(1)} %fusion.33) | copy-start | bytes 2359300
  33.1 6.3 %copy-start.20 = (s32[256,9]{0,1:T(8,128)S(1)}, s32[256,9]{0,1:T(8,128)}, u32[]{:S(2)}) copy-start(s32[256,9]{0,1:T(8,128)} %param.13) | copy-start | bytes 27652
  33.1 6.7 %copy-start.13 = (bf16[1,256,512]{2,1,0:T(8,128)(2,1)S(1)}, bf16[1,256,512]{2,1,0:T(8,128)(2,1)}, u32[]{:S(2)}) copy-start(bf16[1,256,512]{2,1,0:T(8,128)(2,1)} %param.9) | copy-start | bytes 786436
  33.8 26.2 %collective-permute-start.3 = (bf16[2,64,512]{2,1,0:T(8,128)(2,1)}, bf16[2,64,512]{2,1,0:T(8,128)(2,1)}, u32[]{:S(2)}, u32[]{:S(2)}) collective-permute-start(bf16[2,64,512]{2,1,0:T(8,128)(2,1)} %get-tuple-element.39), channel_id=1, source_target_pairs={{0,2},{2,4},{4,6},{6,0},{1,3},{3,5},{5,7},{7,1},{8,10},{10,12},{12... | collective-permute-start | bytes 393224 | tf_op jit(solution)/shard_map/ppermute | solution.py:20
  33.8 26.2 %collective-permute-start.4 = (bf16[2,64,512]{2,1,0:T(8,128)(2,1)}, bf16[2,64,512]{2,1,0:T(8,128)(2,1)}, u32[]{:S(2)}, u32[]{:S(2)}) collective-permute-start(bf16[2,64,512]{2,1,0:T(8,128)(2,1)} %get-tuple-element.40), channel_id=1, source_target_pairs={{2,0},{4,2},{6,4},{0,6},{3,1},{5,3},{7,5},{1,7},{10,8},{12,10},{14... | collective-permute-start | bytes 393224 | tf_op jit(solution)/shard_map/ppermute | solution.py:21
  39.8 41.2 %copy-start.18 = (pred[256,192]{1,0:T(8,128)(4,1)}, pred[256,192]{1,0:T(8,128)(4,1)S(1)}, u32[]{:S(2)}) copy-start(pred[256,192]{1,0:T(8,128)(4,1)S(1)} %copy.103) | copy-start | bytes 147460
  84.5 3.6 copy-start.21
  121.3 1.7 copy-start.9
  121.3 1.7 copy-start.10
  121.3 1.8 copy-start.11
  123.3 1.4 slice-start
  123.5 3.0 copy-start.15
  124.2 11.6 %collective-permute-start.5 = (f32[2,64,512]{2,1,0:T(8,128)}, f32[2,64,512]{2,1,0:T(8,128)}, u32[]{:S(2)}, u32[]{:S(2)}) collective-permute-start(f32[2,64,512]{2,1,0:T(8,128)} %fusion.91), channel_id=1, source_target_pairs={{0,2},{2,4},{4,6},{6,0},{1,3},{3,5},{5,7},{7,1},{8,10},{10,12},{12... | collective-permute-start | bytes 786440 | tf_op jit(solution)/shard_map/ppermute | solution.py:20
  132.6 8.5 %copy-start.22 = (f32[4,8,64]{2,1,0:T(8,128)S(1)}, f32[4,8,64]{2,1,0:T(8,128)}, u32[]{:S(2)}) copy-start(f32[4,8,64]{2,1,0:T(8,128)} %copy-done.21) | copy-start | bytes 24580
  137.7 23.8 %collective-permute-start.6 = (f32[2,64,512]{2,1,0:T(8,128)}, f32[2,64,512]{2,1,0:T(8,128)}, u32[]{:S(2)}, u32[]{:S(2)}) collective-permute-start(f32[2,64,512]{2,1,0:T(8,128)} %get-tuple-element.29), channel_id=1, source_target_pairs={{2,0},{4,2},{6,4},{0,6},{3,1},{5,3},{7,5},{1,7},{10,8},{12,10},{14... | collective-permute-start | bytes 786440 | tf_op jit(solution)/shard_map/ppermute | solution.py:21
  160.3 1.3 copy-start.2
  160.3 1.5 copy-start.4
  161.5 1.3 copy-start.12
  165.5 61.6 %reduce-scatter.4.cloned.1.call-start = ((), (), s32[]{:S(2)}) async-start(), calls=%async_computation.3 | async-start | bytes 1572864 | tf_op jit(solution)/shard_map/reduce_scatter | solution.py:117
  187.1 153.3 %reduce-scatter.6.cloned.1.call-start = ((), (), s32[]{:S(2)}) async-start(), calls=%async_computation.5 | async-start | bytes 7864320 | tf_op jit(solution)/shard_map/reduce_scatter | solution.py:167
  192.1 195.3 %reduce-scatter.8.cloned.1.call-start = ((), (), s32[]{:S(2)}) async-start(), calls=%async_computation.6 | async-start | bytes 2621440 | tf_op jit(solution)/shard_map/reduce_scatter | solution.py:168
  202.4 3.3 copy-start.14
  206.6 34.9 %collective-permute-start.7 = (bf16[256,512]{1,0:T(8,128)(2,1)}, bf16[256,512]{1,0:T(8,128)(2,1)S(1)}, u32[]{:S(2)}, u32[]{:S(2)}) collective-permute-start(bf16[256,512]{1,0:T(8,128)(2,1)} %fusion.74), channel_id=1, source_target_pairs={{0,24},{8,0},{16,8},{24,16},{1,25},{9,1},{17,9},{25,17},{2,26},{10... | collective-permute-start | bytes 786440 | tf_op jit(solution)/shard_map/ppermute | solution.py:29
  229.0 12.4 %collective-permute-start.2 = (bf16[256,512]{1,0:T(8,128)(2,1)}, bf16[256,512]{1,0:T(8,128)(2,1)}, u32[]{:S(2)}, u32[]{:S(2)}) collective-permute-start(bf16[256,512]{1,0:T(8,128)(2,1)} %fusion.75), channel_id=1, source_target_pairs={{0,8},{8,16},{16,24},{24,0},{1,9},{9,17},{17,25},{25,1},{2,10},{10... | collective-permute-start | bytes 786440 | tf_op jit(solution)/shard_map/ppermute | solution.py:29
  (5 other events, 4.2 us)
Sparse Core Ops, SparseCore 0:
  165.6 38.2 all-reduce.7
  206.8 20.3 reduce-scatter.3
  229.5 110.8 reduce-scatter.5
  343.1 44.3 reduce-scatter.7
where the time goes:
time: 398 us; the launch traced here: 396 us
  waiting for transfers between devices  164 us (41%)
  matrix products  77.2 us (19%)
  local copies, waits for them, and re-layouts  70 us (18%)
  blocking collectives  37.5 us (9%)
  other arithmetic  21 us (5%)
  between operations  14.1 us (4%)
  starting transfers between devices  12.4 us (3%)
    reduce_scatter x1, waiting for transfers between devices, shards(): lax.psum_scatter(grad_weights_in, 'patch', scatter_dimension=1, tiled=True)  98.9 us
    reduce_scatter x1, waiting for transfers between devices, shards(): lax.psum_scatter(grad_output, 'patch', scatter_dimension=1, tiled=True)  44.1 us
    reduce_scatter x1, waiting for transfers between devices, shards(): lax.psum_scatter(partial_update, 'tensor', scatter_dimension=1, tiled=True)  19.6 us
    dot_general x1, matrix products, shards(): jnp.einsum('thpq,tphe->tqhe', grad_scores, query_heads, preferred_element...  16.2 us
    dot_general x1, matrix products, shards(): jnp.einsum('thpq,tqhe->tphe', grad_scores, key_heads, preferred_element_t...  15.8 us
    psum x1, blocking collectives, shards(): gain_share = lax.psum(gain_local, 'patch')  12.3 us
    all_gather x1, blocking collectives, shards(): lax.all_gather(forward_input[0], 'tensor', axis=1, tiled=True)  10.3 us
    dot_general x2, matrix products, attend(): jnp.einsum('thpq,tqhe->tphe', rounded, value_heads, preferred_element_typ...  10.3 us
  transfers between devices with their start and end apart: 12, of which 4 were waited for; matrix products, arithmetic and copies ran while one was open for 39% of the time, Pallas kernels for 0%

commit v1 on v0

v1 whole, which is shorter than its diff:
```python
import functools

import jax
import jax.numpy as jnp
from jax import lax
from jax.experimental import pallas as pl
from jax.experimental.pallas import tpu as pltpu
from jax.sharding import PartitionSpec as P

HEAD = 64
HALO = 64
TILE = 128
WINDOW = TILE + 2 * HALO
EPSILON = 1e-06
MESH = pl.DeviceIdType.MESH
F32 = jnp.float32
BF16 = jnp.bfloat16


def mm(a, b):
    return lax.dot_general(a, b, (((1,), (0,)), ((), ())), preferred_element_type=F32)


def mm_nt(a, b):
    return lax.dot_general(a, b, (((1,), (1,)), ((), ())), preferred_element_type=F32)


def mm_tn(a, b):
    return lax.dot_general(a, b, (((0,), (0,)), ((), ())), preferred_element_type=F32)


def kernel(
    n_section, n_patch, turned,
    xf_hbm, xb_hbm, cot_hbm, gain_ref, w_hbm, wo_hbm, near_ref,
    fo_ref, bo_ref, gp_ref, go_ref, gg_ref,
    xf, xb, cot, w, wo, bias, normed_b, normed_f, inverse_ref,
    q_b, q_f, kv_b, kv_f, g, att_b, att_f, grads, kvg, rim_out, rim_in,
    up_own, up_out, up_in, gn_own, gn_out, gn_in, corr_out, corr_in,
    fo_out, bo_out, parts, landed, gain_out, gain_in,
    loc, ts, tr, hs, hr, ss, sr, ws, wr, gs, gr,
):
    s, p, t = lax.axis_index("section"), lax.axis_index("patch"), lax.axis_index("tensor")
    peer = 1 - t
    rows, half = xf_hbm.shape
    width = 2 * half
    chunk = width // n_patch
    total = rows * n_patch
    after = lax.rem(p + 1, n_patch)
    before = lax.rem(p + n_patch - 1, n_patch)
    s_next = lax.rem(s + 1, n_section)
    s_prev = lax.rem(s + n_section - 1, n_section)

    w_copies = [pltpu.make_async_copy(w_hbm.at[c], w.at[c], loc.at[c]) for c in range(3)]
    wo_copy = pltpu.make_async_copy(wo_hbm, wo, loc.at[3])
    xb_copy = pltpu.make_async_copy(xb_hbm, xb.at[t], loc.at[4])
    cot_copy = pltpu.make_async_copy(cot_hbm, cot.at[t], loc.at[5])
    xf_copy = pltpu.make_async_copy(xf_hbm, xf.at[t], loc.at[6])
    for copy in (xb_copy, w_copies[1], w_copies[2], w_copies[0], cot_copy, wo_copy, xf_copy):
        copy.start()

    barrier = pltpu.get_barrier_semaphore()
    pl.semaphore_signal(barrier, inc=1, device_id={"tensor": peer}, device_id_type=MESH)
    pl.semaphore_signal(barrier, inc=1, device_id={"section": s_next}, device_id_type=MESH)
    pl.semaphore_signal(barrier, inc=1, device_id={"section": s_prev}, device_id_type=MESH)

    def greet(k, carry):
        pl.semaphore_signal(
            barrier, inc=1, device_id={"patch": lax.rem(p + k, n_patch)}, device_id_type=MESH
        )
        return carry

    lax.fori_loop(1, n_patch, greet, 0)
    pl.semaphore_wait(barrier, 2 + n_patch)

    def to_peer(i, src, dst):
        return pltpu.make_async_remote_copy(
            src_ref=src, dst_ref=dst, send_sem=ts.at[i], recv_sem=tr.at[i],
            device_id={"tensor": peer}, device_id_type=MESH,
        )

    def to_patch(i, src, dst, where):
        return pltpu.make_async_remote_copy(
            src_ref=src, dst_ref=dst, send_sem=hs.at[i], recv_sem=hr.at[i],
            device_id={"patch": where}, device_id_type=MESH,
        )

    xb_send = to_peer(0, xb_hbm, xb.at[t])
    cot_send = to_peer(1, cot_hbm, cot.at[t])
    xf_send = to_peer(2, xf_hbm, xf.at[t])
    xb_send.start()
    cot_send.start()
    xf_send.start()

    first = p * rows - HALO
    tile_start = lax.broadcasted_iota(jnp.int32, (rows, 1), 0) // TILE * TILE
    place = near_ref[...] - first
    place = jnp.where(place < 0, place + total, place)
    place = jnp.where(place >= total, place - total, place) - tile_start
    column = lax.broadcasted_iota(jnp.int32, (rows, WINDOW), 1)
    seen = jnp.full((rows, WINDOW), -1e30, F32)
    for k in range(near_ref.shape[1]):
        seen = jnp.where(place[:, k : k + 1] == column, 0.0, seen)
    bias[...] = seen

    def normalize(x, normed):
        lo, hi = x[0].astype(F32), x[1].astype(F32)
        square = jnp.sum(lo * lo, axis=-1, keepdims=True) + jnp.sum(hi * hi, axis=-1, keepdims=True)
        inverse = lax.rsqrt(square * (1.0 / width) + EPSILON)
        normed[:, :half] = (lo * inverse * gain_ref[0]).astype(BF16)
        normed[:, half:] = (hi * inverse * gain_ref[1]).astype(BF16)
        return inverse

    def key_value(normed, kv):
        kv[HALO : HALO + rows, :half] = mm(normed[...], w[1]).astype(BF16)
        kv[HALO : HALO + rows, half:] = mm(normed[...], w[2]).astype(BF16)

    def halo(i, kv):
        return (
            to_patch(i, kv.at[pl.ds(HALO, HALO)], kv.at[pl.ds(HALO + rows, HALO)], before),
            to_patch(i + 1, kv.at[pl.ds(rows, HALO)], kv.at[pl.ds(0, HALO)], after),
        )

    xb_copy.wait()
    xb_send.wait_recv()
    inverse_ref[...] = jnp.broadcast_to(normalize(xb, normed_b), inverse_ref.shape)
    w_copies[1].wait()
    w_copies[2].wait()
    key_value(normed_b, kv_b)
    halo_b = halo(0, kv_b)
    for copy in halo_b:
        copy.start()
    w_copies[0].wait()
    q_b[...] = mm(normed_b[...], w[0]).astype(BF16)

    cot_copy.wait()
    wo_copy.wait()
    cot_send.wait_recv()
    g[...] = (mm_nt(cot[0], wo[:, :half]) + mm_nt(cot[1], wo[:, half:])).astype(BF16)

    xf_copy.wait()
    xf_send.wait_recv()
    normalize(xf, normed_f)
    key_value(normed_f, kv_f)
    halo_f = halo(2, kv_f)
    for copy in halo_f:
        copy.start()
    q_f[...] = mm(normed_f[...], w[0]).astype(BF16)

    lane = lax.broadcasted_iota(jnp.int32, (TILE, 2 * HEAD), 1)
    is_low = lane < HEAD
    low = jnp.where(is_low, 1.0, 0.0).astype(BF16)
    high = jnp.where(is_low, 0.0, 1.0).astype(BF16)

    def stacked(x):
        return jnp.concatenate([x * low, x * high], axis=0)

    def unstacked(x):
        return jnp.where(is_low, x[:TILE], x[TILE:])

    pairs = half // (2 * HEAD)
    steps = rows // TILE * pairs
    scale = HEAD ** (-0.5)

    def places(step):
        row = pl.multiple_of(step // pairs * TILE, TILE)
        col = pl.multiple_of(lax.rem(step, pairs) * (2 * HEAD), 2 * HEAD)
        value_col = pl.multiple_of(half + lax.rem(step, pairs) * (2 * HEAD), 2 * HEAD)
        return row, col, value_col

    def weights_of(q, kv, row, col):
        queries = stacked(q[pl.ds(row, TILE), pl.ds(col, 2 * HEAD)])
        keys = kv[pl.ds(row, WINDOW), pl.ds(col, 2 * HEAD)]
        mask = bias[pl.ds(row, TILE), :]
        scores = mm_nt(queries, keys) * scale + jnp.concatenate([mask, mask], axis=0)
        exponent = jnp.exp(scores - jnp.max(scores, axis=-1, keepdims=True))
        weights = exponent * (1.0 / jnp.sum(exponent, axis=-1, keepdims=True))
        return queries, keys, weights

    for copy in halo_b:
        copy.wait_recv()
    kvg[...] = jnp.zeros_like(kvg)

    def backward_step(step, carry):
        row, col, value_col = places(step)
        queries, keys, weights = weights_of(q_b, kv_b, row, col)
        values = kv_b[pl.ds(row, WINDOW), pl.ds(value_col, 2 * HEAD)]
        rounded = weights.astype(BF16)
        here = (pl.ds(row, TILE), pl.ds(col, 2 * HEAD))
        att_b[here] = unstacked(mm(rounded, values)).astype(BF16)
        grad_heads = stacked(g[here])
        grad_weights = mm_nt(grad_heads, values)
        inner = jnp.sum(weights * grad_weights, axis=-1, keepdims=True)
        grad_scores = (weights * (grad_weights - inner) * scale).astype(BF16)
        grads[0, pl.ds(row, TILE), pl.ds(col, 2 * HEAD)] = unstacked(mm(grad_scores, keys)).astype(BF16)
        kvg[pl.ds(row, WINDOW), pl.ds(col, 2 * HEAD)] += mm_tn(grad_scores, queries)
        kvg[pl.ds(row, WINDOW), pl.ds(value_col, 2 * HEAD)] += mm_tn(rounded, grad_heads)
        return carry

    lax.fori_loop(0, steps, backward_step, 0)

    rim_out[0] = kvg[:HALO].astype(BF16)
    rim_out[1] = kvg[HALO + rows :].astype(BF16)
    rims = (
        to_patch(4, rim_out.at[0], rim_in.at[0], before),
        to_patch(5, rim_out.at[1], rim_in.at[1], after),
    )
    for copy in rims:
        copy.start()

    def part_copy(i, k):
        where = lax.rem(p + k, n_patch)
        return pltpu.make_async_remote_copy(
            src_ref=parts.at[i, pl.ds(pl.multiple_of(where * chunk, chunk), chunk)],
            dst_ref=landed.at[i, k], send_sem=ws.at[i, k], recv_sem=wr.at[i, k],
            device_id={"patch": where}, device_id_type=MESH,
        )

    def send_part(i):
        def one(k, carry):
            part_copy(i, k).start()
            return carry

        lax.fori_loop(1, n_patch, one, 0)

    parts[0, :half] = mm_tn(cot[0], att_b[...]).astype(BF16)
    parts[0, half:] = mm_tn(cot[1], att_b[...]).astype(BF16)
    send_part(0)
    parts[1] = mm_tn(normed_b[...], grads[0]).astype(BF16)
    send_part(1)

    for copy in halo_f:
        copy.wait_recv()

    def forward_step(step, carry):
        row, col, value_col = places(step)
        weights = weights_of(q_f, kv_f, row, col)[2]
        values = kv_f[pl.ds(row, WINDOW), pl.ds(value_col, 2 * HEAD)]
        att_f[pl.ds(row, TILE), pl.ds(col, 2 * HEAD)] = unstacked(
            mm(weights.astype(BF16), values)
        ).astype(BF16)
        return carry

    def forward_half(which):
        return mm(att_f[...], wo[:, pl.ds(pl.multiple_of(which * half, half), half)])

    for copy in rims:
        copy.wait_recv()
    kvg[pl.ds(rows, HALO)] += rim_in[0].astype(F32)
    kvg[pl.ds(HALO, HALO)] += rim_in[1].astype(F32)
    grads[1] = kvg[HALO : HALO + rows, :half].astype(BF16)
    grads[2] = kvg[HALO : HALO + rows, half:].astype(BF16)
    parts[2] = mm_tn(normed_b[...], grads[1]).astype(BF16)
    send_part(2)
    parts[3] = mm_tn(normed_b[...], grads[2]).astype(BF16)
    send_part(3)

    inverse = inverse_ref[:, :1]

    def normed_half(which):
        d = pl.ds(pl.multiple_of(which * half, half), half)
        return mm_nt(grads[0], w[0, d]) + mm_nt(grads[1], w[1, d]) + mm_nt(grads[2], w[2, d])

    def unit_half(which):
        return xb[which].astype(F32) * inverse

    away = normed_half(peer)
    gn_out[...] = away.astype(BF16)
    gn_send = to_peer(4, gn_out, gn_in)
    gn_send.start()
    near = normed_half(t)
    gn_own[...] = near
    corr = jnp.sum(away * unit_half(peer) * gain_ref[peer], axis=-1, keepdims=True)
    corr = corr + jnp.sum(near * unit_half(t) * gain_ref[t], axis=-1, keepdims=True)
    corr_row = jnp.broadcast_to(corr, (rows, 128)).T
    corr_out[...] = corr_row[:8]
    corr_send = to_peer(5, corr_out, corr_in)
    corr_send.start()

    lax.fori_loop(0, steps, forward_step, 0)
    up_out[...] = forward_half(peer).astype(BF16)
    up_send = to_peer(3, up_out, up_in)
    up_send.start()
    up_own[...] = forward_half(t)

    gn_send.wait_recv()
    corr_send.wait_recv()
    summed = gn_own[...] + gn_in[...].astype(F32)
    unit = unit_half(t)
    row_sum = jnp.broadcast_to((corr_out[...] + corr_in[...])[:1], (128, rows)).T[:, :1]
    change = inverse * (summed * gain_ref[t] - unit * (row_sum * (1.0 / width)))
    bo_out[...] = (cot[t].astype(F32) + change).astype(BF16)
    bo_send = pltpu.make_async_remote_copy(
        src_ref=bo_out, dst_ref=bo_ref, send_sem=ss.at[0], recv_sem=sr.at[0],
        device_id={"section": s_prev}, device_id_type=MESH,
    )
    bo_send.start()
    gain_own = jnp.sum(summed * unit, axis=0, keepdims=True)
    gain_out[...] = jnp.broadcast_to(gain_own, gain_out.shape)

    def gain_copy(k):
        return pltpu.make_async_remote_copy(
            src_ref=gain_out, dst_ref=gain_in.at[k], send_sem=gs.at[k], recv_sem=gr.at[k],
            device_id={"patch": lax.rem(p + k, n_patch)}, device_id_type=MESH,
        )

    def gain_start(k, carry):
        gain_copy(k).start()
        return carry

    lax.fori_loop(1, n_patch, gain_start, 0)

    up_send.wait_recv()
    fo_out[...] = (xf[t].astype(F32) + up_own[...] + up_in[...].astype(F32)).astype(BF16)
    fo_send = pltpu.make_async_remote_copy(
        src_ref=fo_out, dst_ref=fo_ref, send_sem=ss.at[1], recv_sem=sr.at[1],
        device_id={"section": s_next}, device_id_type=MESH,
    )
    fo_send.start()

    def gain_end(k, total_gain):
        copy = gain_copy(k)
        copy.wait_send()
        copy.wait_recv()
        return total_gain + gain_in[k]

    gg_ref[...] = lax.fori_loop(1, n_patch, gain_end, gain_out[...])

    own = pl.ds(pl.multiple_of(p * chunk, chunk), chunk)
    for i in range(4):
        def part_end(k, total_part):
            copy = part_copy(i, k)
            copy.wait_send()
            copy.wait_recv()
            gp_ref_i[...] += landed[i, k].astype(F32)
            return total_part

        gp_ref_i = gp_ref.at[i - 1] if i > 0 else (gn_own.at[pl.ds(0, chunk)] if turned else go_ref)
        gp_ref_i[...] = parts[i, own].astype(F32)
        lax.fori_loop(1, n_patch, part_end, 0)
    if turned:
        go_ref[...] = gn_own[:chunk].T

    for copy in (xb_send, cot_send, xf_send, gn_send, corr_send, up_send):
        copy.wait_send()
    for copy in halo_b + halo_f + rims:
        copy.wait_send()
    bo_send.wait()
    fo_send.wait()


def shards(n_section, n_patch, xf, xb, cot, norm_gain, projection, output_weight, neighbours):
    rows, half = xf.shape[1:]
    width = 2 * half
    chunk = width // n_patch
    turned = chunk % 128 == 0
    anywhere = pl.BlockSpec(memory_space=pl.ANY)
    vmem = pl.BlockSpec(memory_space=pltpu.VMEM)
    block = lambda *shape, dtype=BF16: pltpu.VMEM(shape, dtype)
    dma = pltpu.SemaphoreType.DMA
    outs = pl.pallas_call(
        functools.partial(kernel, n_section, n_patch, turned),
        out_shape=(
            jax.ShapeDtypeStruct((rows, half), BF16),
            jax.ShapeDtypeStruct((rows, half), BF16),
            jax.ShapeDtypeStruct((3, chunk, half), F32),
            jax.ShapeDtypeStruct((half, chunk) if turned else (chunk, half), F32),
            jax.ShapeDtypeStruct((8, half), F32),
        ),
        in_specs=[anywhere, anywhere, anywhere, vmem, anywhere, anywhere, vmem],
        out_specs=(anywhere, anywhere, vmem, vmem, vmem),
        scratch_shapes=[
            block(2, rows, half), block(2, rows, half), block(2, rows, half),
            block(3, width, half), block(half, width), block(rows, WINDOW, dtype=F32),
            block(rows, width), block(rows, width), block(rows, 128, dtype=F32),
            block(rows, half), block(rows, half),
            block(rows + 2 * HALO, width), block(rows + 2 * HALO, width),
            block(rows, half), block(rows, half), block(rows, half), block(3, rows, half),
            block(rows + 2 * HALO, width, dtype=F32), block(2, HALO, width), block(2, HALO, width),
            block(rows, half, dtype=F32), block(rows, half), block(rows, half),
            block(rows, half, dtype=F32), block(rows, half), block(rows, half),
            block(8, rows, dtype=F32), block(8, rows, dtype=F32),
            block(rows, half), block(rows, half),
            block(4, width, half), block(4, n_patch, chunk, half),
            block(8, half, dtype=F32), block(n_patch, 8, half, dtype=F32),
            dma((7,)), dma((6,)), dma((6,)), dma((6,)), dma((6,)), dma((2,)), dma((2,)),
            dma((4, n_patch)), dma((4, n_patch)), dma((n_patch,)), dma((n_patch,)),
        ],
        compiler_params=pltpu.CompilerParams(
            collective_id=0, has_side_effects=True, vmem_limit_bytes=56 * 2**20
        ),
        cost_estimate=pl.CostEstimate(flops=6 * 10**9, bytes_accessed=8 * 2**20, transcendentals=10**6),
    )(
        xf[0], xb[0], cot[0], norm_gain[0].reshape(2, 1, half), projection[0], output_weight[0],
        neighbours,
    )
    forward, backward, grad_projection, grad_output, gain = outs
    if not turned:
        grad_output = grad_output.T
    return forward[None], backward[None], grad_projection[None], grad_output[None], gain[:1]


def solution(mesh):
    return jax.shard_map(
        functools.partial(shards, mesh.shape["section"], mesh.shape["patch"]),
        mesh=mesh,
        in_specs=(
            P("section", "patch", "tensor"),
            P("section", "patch", "tensor"),
            P("section", "patch", "tensor"),
            P("section", None),
            P("section", None, None, "tensor"),
            P("section", "tensor", None),
            P("patch", None),
        ),
        out_specs=(
            P("section", "patch", "tensor"),
            P("section", "patch", "tensor"),
            P("section", None, "patch", "tensor"),
            P("section", "tensor", "patch"),
            P("section", "tensor"),
        ),
        check_vma=False,
    )
```

time: 398 us -> 146 us (0.37)
  waiting for transfers between devices: 164 us -> 0 us
  Pallas kernels: 0 us -> 135 us
  matrix products: 77.2 us -> 0 us
  local copies, waits for them, and re-layouts: 70 us -> 9.64 us
  blocking collectives: 37.5 us -> 0 us
  other arithmetic: 21 us -> 0 us
  between operations: 14.1 us -> 0.64 us
  starting transfers between devices: 12.4 us -> 0 us
    reduce_scatter x3 -> x0, waiting for transfers between devices: 163 us -> none  [the longest x1 98.9 us: shards(): lax.psum_scatter(grad_weights_in, 'patch', scatter_dimension=1, tiled=True)]
    pallas_call x0 -> x1, Pallas kernels: none -> 135 us  [shards(): pl.pallas_call(functools.partial(kernel, n_section, n_patch, turned), out...]
    dot_general x14 -> x0, matrix products: 70.2 us -> none  [the longest x1 16.2 us: shards(): jnp.einsum('thpq,tphe->tqhe', grad_scores, query_heads, preferred_element...]
    another operation x12 -> x0, local copies, waits for them, and re-layouts: 32.3 us -> none  [the longest x3 9.14 us: attend(): banded(spread_rows[1]).reshape(tiles, 3 * HALO, local_heads, HEAD)]
    all_gather x3 -> x0, blocking collectives: 25.1 us -> none  [the longest x1 10.3 us: shards(): lax.all_gather(forward_input[0], 'tensor', axis=1, tiled=True)]
    psum x1 -> x0, blocking collectives: 12.3 us -> none  [shards(): gain_share = lax.psum(gain_local, 'patch')]
    ppermute x8 -> x0, starting transfers between devices: 12 us -> none  [the longest x3 9.25 us: padded(): after = lax.ppermute(first, axis, down)]
    another operation x8 -> x0, other arithmetic: 11.7 us -> none  [the longest x4 6.89 us: banded(): jnp.stack([blocks[:-2], blocks[1:-1], blocks[2:]], axis=1)]
  transfers between devices with their start and end apart: 12 -> 0, of which waited for: 4 -> 0; matrix products, arithmetic and copies ran while one was open for 39% -> 0% of each run, Pallas kernels for 0% -> 0%
where the time goes in v1:
time: 146 us; the launch traced here: 145 us
  Pallas kernels  135 us (92%)
  local copies, waits for them, and re-layouts  9.64 us (7%)
    pallas_call x1, Pallas kernels, shards(): pl.pallas_call(functools.partial(kernel, n_section, n_patch, turned), out...  135 us
    unnamed x7, local copies, waits for them, and re-layouts  8.34 us

profile of v1, /device:TPU:0, one launch (start us, length us, event | category | flops | bytes accessed | tf_op | source)
XLA Modules:
  0.0 145.5 jit_solution(2697323076184382077)
XLA Ops:
  0.6 1.5 %copy.12.near_ref = s32[256,9]{1,0:T(8,128)} copy(s32[256,9]{0,1:T(8,128)} %param.13) | data formatting | bytes 18432 | tf_op args[6]
  2.1 135.2 %shard_map.110 = (bf16[256,512]{1,0:T(8,128)(2,1)}, bf16[256,512]{1,0:T(8,128)(2,1)}, f32[3,256,512]{2,1,0:T(8,128)}, f32[512,256]{1,0:T(8,128)}, f32[8,512]{1,0:T(8,128)}) custom-call(bf16[256,512]{1,0:T(8,128)(2,1)} %bitcast.16, bf16[256,512]{1,0:T(8,128)(2,1)} %bitcast.17, bf16[256,512]{1,0:T(8,128)(2,1)} %bitcast.18, f32[2,1,512]{2,1,0:T(1,128)} %bitcast.19, ...), custom_call_target="tpu_custom_call" | custom-call | flops 6000000000 | bytes 8388608 | tf_op jit(solution)/shard_map/pallas_call | solution.py:360
  137.3 1.3 slice.3
  138.6 1.7 %copy.17 = bf16[1,256,512]{2,1,0:T(8,128)(2,1)} copy(bf16[1,256,512]{2,1,0:T(8,128)(2,1)} %bitcast.13) | data formatting | bytes 524288
  140.3 1.7 %copy.18 = bf16[1,256,512]{2,1,0:T(8,128)(2,1)} copy(bf16[1,256,512]{2,1,0:T(8,128)(2,1)} %bitcast.12) | data formatting | bytes 524288
  141.9 0.0 copy-start
  141.9 2.7 %copy.19 = f32[1,3,256,512]{3,2,1,0:T(8,128)} copy(f32[1,3,256,512]{3,2,1,0:T(8,128)} %bitcast.10) | data formatting | bytes 3145728
  144.7 0.0 copy-done
  144.7 0.8 copy.20
Async XLA Ops:
  141.9 2.7 %copy-start = (f32[512,256]{1,0:T(8,128)S(1)}, f32[512,256]{1,0:T(8,128)}, u32[]{:S(2)}) copy-start(f32[512,256]{1,0:T(8,128)} %get-tuple-element.13) | copy-start | bytes 1572868

commit v2 on v1

--- a/solution.py
+++ b/solution.py
@@ -34,10 +34,10 @@
     xf_hbm, xb_hbm, cot_hbm, gain_ref, w_hbm, wo_hbm, near_ref,
     fo_ref, bo_ref, gp_ref, go_ref, gg_ref,
     xf, xb, cot, w, wo, bias, normed_b, normed_f, inverse_ref,
-    q_b, q_f, kv_b, kv_f, g, att_b, att_f, grads, kvg, rim_out, rim_in,
+    q_b, q_f, kv_b, kv_f, g, att_b, att_f, grad_q, kvg, rim_out, rim_in,
     up_own, up_out, up_in, gn_own, gn_out, gn_in, corr_out, corr_in,
-    fo_out, bo_out, parts, landed, gain_out, gain_in,
-    loc, ts, tr, hs, hr, ss, sr, ws, wr, gs, gr,
+    fo_out, bo_out, parts, landed, gain_out, gain_in, near, turned_b, columns, gathered,
+    loc, ts, tr, hs, hr, ss, sr, rs_s, rs_r, ag_s, ag_r, ns, nr, gs, gr,
 ):
     s, p, t = lax.axis_index("section"), lax.axis_index("patch"), lax.axis_index("tensor")
     peer = 1 - t
@@ -88,17 +88,17 @@
     cot_send = to_peer(1, cot_hbm, cot.at[t])
     xf_send = to_peer(2, xf_hbm, xf.at[t])
     xb_send.start()
-    cot_send.start()
-    xf_send.start()
 
     first = p * rows - HALO
     tile_start = lax.broadcasted_iota(jnp.int32, (rows, 1), 0) // TILE * TILE
-    place = near_ref[...] - first
+    near[...] = jnp.zeros_like(near)
+    near[: near_ref.shape[0], :] = near_ref[...].astype(F32)
+    place = near[...].T.astype(jnp.int32) - first
     place = jnp.where(place < 0, place + total, place)
     place = jnp.where(place >= total, place - total, place) - tile_start
     column = lax.broadcasted_iota(jnp.int32, (rows, WINDOW), 1)
     seen = jnp.full((rows, WINDOW), -1e30, F32)
-    for k in range(near_ref.shape[1]):
+    for k in range(near_ref.shape[0]):
         seen = jnp.where(place[:, k : k + 1] == column, 0.0, seen)
     bias[...] = seen
 
@@ -122,6 +122,7 @@
 
     xb_copy.wait()
     xb_send.wait_recv()
+    cot_send.start()
     inverse_ref[...] = jnp.broadcast_to(normalize(xb, normed_b), inverse_ref.shape)
     w_copies[1].wait()
     w_copies[2].wait()
@@ -135,16 +136,9 @@
     cot_copy.wait()
     wo_copy.wait()
     cot_send.wait_recv()
+    xf_send.start()
+    turned_b[...] = normed_b[...].T
     g[...] = (mm_nt(cot[0], wo[:, :half]) + mm_nt(cot[1], wo[:, half:])).astype(BF16)
-
-    xf_copy.wait()
-    xf_send.wait_recv()
-    normalize(xf, normed_f)
-    key_value(normed_f, kv_f)
-    halo_f = halo(2, kv_f)
-    for copy in halo_f:
-        copy.start()
-    q_f[...] = mm(normed_f[...], w[0]).astype(BF16)
 
     lane = lax.broadcasted_iota(jnp.int32, (TILE, 2 * HEAD), 1)
     is_low = lane < HEAD
@@ -179,6 +173,23 @@
     for copy in halo_b:
         copy.wait_recv()
     kvg[...] = jnp.zeros_like(kvg)
+
+    def rows_of(c):
+        return pl.ds(pl.multiple_of(c * chunk, chunk), chunk)
+
+    def columns_copy(where, source):
+        return pltpu.make_async_remote_copy(
+            src_ref=turned_b.at[rows_of(where)], dst_ref=columns.at[source],
+            send_sem=ns.at[where], recv_sem=nr.at[source],
+            device_id={"patch": where}, device_id_type=MESH,
+        )
+
+    def columns_start(k, carry):
+        columns_copy(lax.rem(p + k, n_patch), p).start()
+        return carry
+
+    lax.fori_loop(1, n_patch, columns_start, 0)
+    columns[p] = turned_b[rows_of(p)]
 
     def backward_step(step, carry):
         row, col, value_col = places(step)
@@ -191,7 +202,7 @@
         grad_weights = mm_nt(grad_heads, values)
         inner = jnp.sum(weights * grad_weights, axis=-1, keepdims=True)
         grad_scores = (weights * (grad_weights - inner) * scale).astype(BF16)
-        grads[0, pl.ds(row, TILE), pl.ds(col, 2 * HEAD)] = unstacked(mm(grad_scores, keys)).astype(BF16)
+        grad_q[here] = unstacked(mm(grad_scores, keys)).astype(BF16)
         kvg[pl.ds(row, WINDOW), pl.ds(col, 2 * HEAD)] += mm_tn(grad_scores, queries)
         kvg[pl.ds(row, WINDOW), pl.ds(value_col, 2 * HEAD)] += mm_tn(rounded, grad_heads)
         return carry
@@ -207,29 +218,106 @@
     for copy in rims:
         copy.start()
 
-    def part_copy(i, k):
-        where = lax.rem(p + k, n_patch)
+    def sum_copy(d, i, c):
         return pltpu.make_async_remote_copy(
-            src_ref=parts.at[i, pl.ds(pl.multiple_of(where * chunk, chunk), chunk)],
-            dst_ref=landed.at[i, k], send_sem=ws.at[i, k], recv_sem=wr.at[i, k],
-            device_id={"patch": where}, device_id_type=MESH,
-        )
-
-    def send_part(i):
-        def one(k, carry):
-            part_copy(i, k).start()
-            return carry
-
-        lax.fori_loop(1, n_patch, one, 0)
+            src_ref=parts.at[i, rows_of(c)], dst_ref=landed.at[d, i, c],
+            send_sem=rs_s.at[d, i, c], recv_sem=rs_r.at[d, i, c],
+            device_id={"patch": before if d else after}, device_id_type=MESH,
+        )
+
+    def sums_first(i):
+        @pl.when(p == 0)
+        def _():
+            def one(k, carry):
+                sum_copy(0, i, n_patch - k).start()
+                return carry
+
+            lax.fori_loop(1, n_patch, one, 0)
+
+        @pl.when(p == n_patch - 1)
+        def _():
+            def one(k, carry):
+                sum_copy(1, i, k).start()
+                return carry
+
+            lax.fori_loop(0, n_patch - 1, one, 0)
+
+    def sums_stage(m):
+        right, left = n_patch - 1 - m, m
+
+        def pass_on(d, c):
+            for i in range(2):
+                copy = sum_copy(d, i, c)
+                copy.wait_recv()
+                parts[i, rows_of(c)] = (
+                    parts[i, rows_of(c)].astype(F32) + landed[d, i, c].astype(F32)
+                ).astype(BF16)
+                copy.start()
+
+        @pl.when((right > p) & (p > 0))
+        def _():
+            pass_on(0, right)
+
+        @pl.when((left < p) & (p < n_patch - 1))
+        def _():
+            pass_on(1, left)
+
+    def block_copy(d, i, j):
+        return pltpu.make_async_remote_copy(
+            src_ref=gathered.at[i, j], dst_ref=gathered.at[i, j],
+            send_sem=ag_s.at[d, i, j], recv_sem=ag_r.at[i, j],
+            device_id={"patch": before if d else after}, device_id_type=MESH,
+        )
+
+    def block_start(i, j, goes_right, goes_left):
+        if goes_right:
+            @pl.when(p < n_patch - 1)
+            def _():
+                block_copy(0, i, j).start()
+        if goes_left:
+            @pl.when(p > 0)
+            def _():
+                block_copy(1, i, j).start()
+
+    def blocks_stage(m):
+        left, right = p - 1 - m, p + 1 + m
+
+        @pl.when(left >= 0)
+        def _():
+            for i in range(2):
+                block_copy(0, i, left).wait_recv()
+                block_start(i, left, True, False)
+
+        @pl.when(right < n_patch)
+        def _():
+            for i in range(2):
+                block_copy(1, i, right).wait_recv()
+                block_start(i, right, False, True)
+
+        @pl.when(left >= 0)
+        def _():
+            for i in range(2):
+                gp_ref[1 + i] += mm(columns[left], gathered[i, left])
+
+        @pl.when(right < n_patch)
+        def _():
+            for i in range(2):
+                gp_ref[1 + i] += mm(columns[right], gathered[i, right])
 
     parts[0, :half] = mm_tn(cot[0], att_b[...]).astype(BF16)
     parts[0, half:] = mm_tn(cot[1], att_b[...]).astype(BF16)
-    send_part(0)
-    parts[1] = mm_tn(normed_b[...], grads[0]).astype(BF16)
-    send_part(1)
-
+    sums_first(0)
+    parts[1] = mm(turned_b[...], grad_q[...]).astype(BF16)
+    sums_first(1)
+
+    xf_copy.wait()
+    xf_send.wait_recv()
+    normalize(xf, normed_f)
+    key_value(normed_f, kv_f)
+    halo_f = halo(2, kv_f)
     for copy in halo_f:
-        copy.wait_recv()
+        copy.start()
+    q_f[...] = mm(normed_f[...], w[0]).astype(BF16)
 
     def forward_step(step, carry):
         row, col, value_col = places(step)
@@ -247,18 +335,20 @@
         copy.wait_recv()
     kvg[pl.ds(rows, HALO)] += rim_in[0].astype(F32)
     kvg[pl.ds(HALO, HALO)] += rim_in[1].astype(F32)
-    grads[1] = kvg[HALO : HALO + rows, :half].astype(BF16)
-    grads[2] = kvg[HALO : HALO + rows, half:].astype(BF16)
-    parts[2] = mm_tn(normed_b[...], grads[1]).astype(BF16)
-    send_part(2)
-    parts[3] = mm_tn(normed_b[...], grads[2]).astype(BF16)
-    send_part(3)
+    gathered[0, p] = kvg[HALO : HALO + rows, :half].astype(BF16)
+    block_start(0, p, True, True)
+    gathered[1, p] = kvg[HALO : HALO + rows, half:].astype(BF16)
+    block_start(1, p, True, True)
 
     inverse = inverse_ref[:, :1]
 
     def normed_half(which):
         d = pl.ds(pl.multiple_of(which * half, half), half)
-        return mm_nt(grads[0], w[0, d]) + mm_nt(grads[1], w[1, d]) + mm_nt(grads[2], w[2, d])
+        return (
+            mm_nt(grad_q[...], w[0, d])
+            + mm_nt(gathered[0, p], w[1, d])
+            + mm_nt(gathered[1, p], w[2, d])
+        )
 
     def unit_half(which):
         return xb[which].astype(F32) * inverse
@@ -267,16 +357,30 @@
     gn_out[...] = away.astype(BF16)
     gn_send = to_peer(4, gn_out, gn_in)
     gn_send.start()
-    near = normed_half(t)
-    gn_own[...] = near
+    held = normed_half(t)
+    gn_own[...] = held
     corr = jnp.sum(away * unit_half(peer) * gain_ref[peer], axis=-1, keepdims=True)
-    corr = corr + jnp.sum(near * unit_half(t) * gain_ref[t], axis=-1, keepdims=True)
+    corr = corr + jnp.sum(held * unit_half(t) * gain_ref[t], axis=-1, keepdims=True)
     corr_row = jnp.broadcast_to(corr, (rows, 128)).T
     corr_out[...] = corr_row[:8]
     corr_send = to_peer(5, corr_out, corr_in)
     corr_send.start()
 
-    lax.fori_loop(0, steps, forward_step, 0)
+    def columns_end(k, carry):
+        columns_copy(lax.rem(p + k, n_patch), lax.rem(p + k, n_patch)).wait_recv()
+        return carry
+
+    lax.fori_loop(1, n_patch, columns_end, 0)
+    for i in range(2):
+        gp_ref[1 + i] = mm(columns[p], gathered[i, p])
+
+    sums_stage(0)
+    for copy in halo_f:
+        copy.wait_recv()
+    lax.fori_loop(0, steps // 2, forward_step, 0)
+    sums_stage(1)
+    blocks_stage(0)
+    lax.fori_loop(steps // 2, steps, forward_step, 0)
     up_out[...] = forward_half(peer).astype(BF16)
     up_send = to_peer(3, up_out, up_in)
     up_send.start()
@@ -317,28 +421,68 @@
     )
     fo_send.start()
 
+    def stage(m, carry):
+        @pl.when(m + 1 < n_patch - 1)
+        def _():
+            sums_stage(m + 1)
+
+        blocks_stage(m)
+        return carry
+
+    lax.fori_loop(1, n_patch - 1, stage, 0)
+
     def gain_end(k, total_gain):
         copy = gain_copy(k)
         copy.wait_send()
         copy.wait_recv()
         return total_gain + gain_in[k]
 
-    gg_ref[...] = lax.fori_loop(1, n_patch, gain_end, gain_out[...])
-
-    own = pl.ds(pl.multiple_of(p * chunk, chunk), chunk)
-    for i in range(4):
-        def part_end(k, total_part):
-            copy = part_copy(i, k)
-            copy.wait_send()
-            copy.wait_recv()
-            gp_ref_i[...] += landed[i, k].astype(F32)
-            return total_part
-
-        gp_ref_i = gp_ref.at[i - 1] if i > 0 else (gn_own.at[pl.ds(0, chunk)] if turned else go_ref)
-        gp_ref_i[...] = parts[i, own].astype(F32)
-        lax.fori_loop(1, n_patch, part_end, 0)
+    gg_ref[...] = lax.fori_loop(1, n_patch, gain_end, gain_out[...])[:1]
+
+    for i in range(2):
+        held = gp_ref.at[0] if i == 1 else (gn_own.at[pl.ds(0, chunk)] if turned else go_ref)
+        held[...] = parts[i, rows_of(p)].astype(F32)
+
+        @pl.when(p > 0)
+        def _():
+            sum_copy(0, i, p).wait_recv()
+            held[...] += landed[0, i, p].astype(F32)
+
+        @pl.when(p < n_patch - 1)
+        def _():
+            sum_copy(1, i, p).wait_recv()
+            held[...] += landed[1, i, p].astype(F32)
+
     if turned:
         go_ref[...] = gn_own[:chunk].T
+
+    def sent(k, carry):
+        where = lax.rem(p + k, n_patch)
+        columns_copy(where, p).wait_send()
+        return carry
+
+    lax.fori_loop(1, n_patch, sent, 0)
+
+    def passed(c, carry):
+        for i in range(2):
+            @pl.when((c > p))
+            def _():
+                sum_copy(0, i, c).wait_send()
+
+            @pl.when((c < p))
+            def _():
+                sum_copy(1, i, c).wait_send()
+
+            @pl.when((c <= p) & (p < n_patch - 1))
+            def _():
+                block_copy(0, i, c).wait_send()
+
+            @pl.when((c >= p) & (p > 0))
+            def _():
+                block_copy(1, i, c).wait_send()
+        return carry
+
+    lax.fori_loop(0, n_patch, passed, 0)
 
     for copy in (xb_send, cot_send, xf_send, gn_send, corr_send, up_send):
         copy.wait_send()
@@ -346,6 +490,27 @@
         copy.wait_send()
     bo_send.wait()
     fo_send.wait()
+
+
+def move(*refs):
+    count = len(refs) // 2
+    sources, targets, sems = refs[:count], refs[count : 2 * count], refs[-1]
+    copies = [pltpu.make_async_copy(sources[i], targets[i], sems.at[i]) for i in range(count)]
+    for copy in copies:
+        copy.start()
+    for copy in copies:
+        copy.wait()
+
+
+def hand_out(arrays):
+    anywhere = pl.BlockSpec(memory_space=pl.ANY)
+    return pl.pallas_call(
+        move,
+        out_shape=tuple(jax.ShapeDtypeStruct(a.shape, a.dtype) for a in arrays),
+        in_specs=[anywhere] * len(arrays),
+        out_specs=(anywhere,) * len(arrays),
+        scratch_shapes=[pltpu.SemaphoreType.DMA((len(arrays),))],
+    )(*arrays)
 
 
 def shards(n_section, n_patch, xf, xb, cot, norm_gain, projection, output_weight, neighbours):
@@ -364,7 +529,7 @@
             jax.ShapeDtypeStruct((rows, half), BF16),
             jax.ShapeDtypeStruct((3, chunk, half), F32),
             jax.ShapeDtypeStruct((half, chunk) if turned else (chunk, half), F32),
-            jax.ShapeDtypeStruct((8, half), F32),
+            jax.ShapeDtypeStruct((1, half), F32),
         ),
         in_specs=[anywhere, anywhere, anywhere, vmem, anywhere, anywhere, vmem],
         out_specs=(anywhere, anywhere, vmem, vmem, vmem),
@@ -374,16 +539,19 @@
             block(rows, width), block(rows, width), block(rows, 128, dtype=F32),
             block(rows, half), block(rows, half),
             block(rows + 2 * HALO, width), block(rows + 2 * HALO, width),
-            block(rows, half), block(rows, half), block(rows, half), block(3, rows, half),
+            block(rows, half), block(rows, half), block(rows, half), block(rows, half),
             block(rows + 2 * HALO, width, dtype=F32), block(2, HALO, width), block(2, HALO, width),
             block(rows, half, dtype=F32), block(rows, half), block(rows, half),
             block(rows, half, dtype=F32), block(rows, half), block(rows, half),
             block(8, rows, dtype=F32), block(8, rows, dtype=F32),
             block(rows, half), block(rows, half),
-            block(4, width, half), block(4, n_patch, chunk, half),
+            block(2, width, half), block(2, 2, n_patch, chunk, half),
             block(8, half, dtype=F32), block(n_patch, 8, half, dtype=F32),
+            block(128, rows, dtype=F32), block(width, rows), block(n_patch, chunk, rows),
+            block(2, n_patch, rows, half),
             dma((7,)), dma((6,)), dma((6,)), dma((6,)), dma((6,)), dma((2,)), dma((2,)),
-            dma((4, n_patch)), dma((4, n_patch)), dma((n_patch,)), dma((n_patch,)),
+            dma((2, 2, n_patch)), dma((2, 2, n_patch)), dma((2, 2, n_patch)), dma((2, n_patch)),
+            dma((n_patch,)), dma((n_patch,)), dma((n_patch,)), dma((n_patch,)),
         ],
         compiler_params=pltpu.CompilerParams(
             collective_id=0, has_side_effects=True, vmem_limit_bytes=56 * 2**20
@@ -391,12 +559,13 @@
         cost_estimate=pl.CostEstimate(flops=6 * 10**9, bytes_accessed=8 * 2**20, transcendentals=10**6),
     )(
         xf[0], xb[0], cot[0], norm_gain[0].reshape(2, 1, half), projection[0], output_weight[0],
-        neighbours,
+        neighbours.T,
     )
+    outs = hand_out(outs)
     forward, backward, grad_projection, grad_output, gain = outs
     if not turned:
         grad_output = grad_output.T
-    return forward[None], backward[None], grad_projection[None], grad_output[None], gain[:1]
+    return forward[None], backward[None], grad_projection[None], grad_output[None], gain
 
 
 def solution(mesh):

time: 146 us -> 198 us (1.36)
  Pallas kernels: 135 us -> 197 us
  local copies, waits for them, and re-layouts: 9.64 us -> 0 us
    pallas_call x0 -> x1, Pallas kernels: none -> 80.6 us  [hand_out(): pl.pallas_call(move, out_shape=tuple((jax.ShapeDtypeStruct(a.shape, a.dty...]
    pallas_call x1, Pallas kernels: 135 us -> 117 us  [shards(): pl.pallas_call(functools.partial(kernel, n_section, n_patch, turned), out...]
    unnamed x7 -> x0, local copies, waits for them, and re-layouts: 8.34 us -> none
where the time goes in v2:
time: 198 us
  Pallas kernels  197 us (99%)
    pallas_call x1, Pallas kernels, shards(): pl.pallas_call(functools.partial(kernel, n_section, n_patch, turned), out...  117 us
    pallas_call x1, Pallas kernels, hand_out(): pl.pallas_call(move, out_shape=tuple((jax.ShapeDtypeStruct(a.shape, a.dty...  80.6 us

profile of v2, /device:TPU:0, one launch (start us, length us, event | category | flops | bytes accessed | tf_op | source)
XLA Modules:
  0.0 197.9 jit_solution(15572798161271095739)
XLA Ops:
  0.6 116.6 %shard_map.110 = (bf16[256,512]{1,0:T(8,128)(2,1)}, bf16[256,512]{1,0:T(8,128)(2,1)}, f32[3,256,512]{2,1,0:T(8,128)}, f32[512,256]{1,0:T(8,128)}, f32[1,512]{1,0:T(1,128)}) custom-call(bf16[256,512]{1,0:T(8,128)(2,1)} %bitcast.15, bf16[256,512]{1,0:T(8,128)(2,1)} %bitcast.16, bf16[256,512]{1,0:T(8,128)(2,1)} %bitcast.17, f32[2,1,512]{2,1,0:T(1,128)} %bitcast.21, ...), custom_call_target="tpu_custom_call" | custom-call | flops 6000000000 | bytes 8388608 | tf_op jit(solution)/shard_map/pallas_call | solution.py:525
  117.2 80.6 %shard_map.111 = (bf16[256,512]{1,0:T(8,128)(2,1)}, bf16[256,512]{1,0:T(8,128)(2,1)}, f32[3,256,512]{2,1,0:T(8,128)}, f32[512,256]{1,0:T(8,128)}, f32[1,512]{1,0:T(1,128)}) custom-call(bf16[256,512]{1,0:T(8,128)(2,1)} %get-tuple-element.15.refs_0_, bf16[256,512]{1,0:T(8,128)(2,1)} %get-tuple-element.16.refs_1_, f32[3,256,512]{2,1,0:T(8,128)} %get-tuple-element.17.refs_2_, ...), custom_call_target="tpu_custom_call" | custom-call | tf_op jit(solution)/shard_map/pallas_call | solution.py:507

commit v3 on v2

--- a/solution.py
+++ b/solution.py
@@ -493,12 +493,16 @@
 
 
 def move(*refs):
-    count = len(refs) // 2
-    sources, targets, sems = refs[:count], refs[count : 2 * count], refs[-1]
-    copies = [pltpu.make_async_copy(sources[i], targets[i], sems.at[i]) for i in range(count)]
-    for copy in copies:
+    count = len(refs) // 3
+    sources, targets, held, sems = refs[:count], refs[count : 2 * count], refs[2 * count : -1], refs[-1]
+    ins = [pltpu.make_async_copy(sources[i], held[i], sems.at[0, i]) for i in range(count)]
+    outs = [pltpu.make_async_copy(held[i], targets[i], sems.at[1, i]) for i in range(count)]
+    for copy in ins:
         copy.start()
-    for copy in copies:
+    for i in range(count):
+        ins[i].wait()
+        outs[i].start()
+    for copy in outs:
         copy.wait()
 
 
@@ -509,7 +513,10 @@
         out_shape=tuple(jax.ShapeDtypeStruct(a.shape, a.dtype) for a in arrays),
         in_specs=[anywhere] * len(arrays),
         out_specs=(anywhere,) * len(arrays),
-        scratch_shapes=[pltpu.SemaphoreType.DMA((len(arrays),))],
+        scratch_shapes=[
+            *(pltpu.VMEM(a.shape, a.dtype) for a in arrays),
+            pltpu.SemaphoreType.DMA((2, len(arrays))),
+        ],
     )(*arrays)
 
 

time: 198 us -> 120 us (0.61)
  Pallas kernels: 197 us -> 120 us
    pallas_call x1, Pallas kernels: 80.6 us -> 2.98 us  [hand_out(): pl.pallas_call(move, out_shape=tuple((jax.ShapeDtypeStruct(a.shape, a.dty...]
where the time goes in v3:
time: 120 us
  Pallas kernels  120 us (100%)
    pallas_call x1, Pallas kernels, shards(): pl.pallas_call(functools.partial(kernel, n_section, n_patch, turned), out...  117 us
    pallas_call x1, Pallas kernels, hand_out(): pl.pallas_call(move, out_shape=tuple((jax.ShapeDtypeStruct(a.shape, a.dty...  2.98 us

profile of v3, /device:TPU:0, one launch (start us, length us, event | category | flops | bytes accessed | tf_op | source)
XLA Modules:
  0.0 120.2 jit_solution(11986523591461240491)
XLA Ops:
  0.6 116.6 %shard_map.110 = (bf16[256,512]{1,0:T(8,128)(2,1)}, bf16[256,512]{1,0:T(8,128)(2,1)}, f32[3,256,512]{2,1,0:T(8,128)}, f32[512,256]{1,0:T(8,128)}, f32[1,512]{1,0:T(1,128)}) custom-call(bf16[256,512]{1,0:T(8,128)(2,1)} %bitcast.15, bf16[256,512]{1,0:T(8,128)(2,1)} %bitcast.16, bf16[256,512]{1,0:T(8,128)(2,1)} %bitcast.17, f32[2,1,512]{2,1,0:T(1,128)} %bitcast.21, ...), custom_call_target="tpu_custom_call" | custom-call | flops 6000000000 | bytes 8388608 | tf_op jit(solution)/shard_map/pallas_call | solution.py:532
  117.2 3.0 %shard_map.111 = (bf16[256,512]{1,0:T(8,128)(2,1)}, bf16[256,512]{1,0:T(8,128)(2,1)}, f32[3,256,512]{2,1,0:T(8,128)}, f32[512,256]{1,0:T(8,128)}, f32[1,512]{1,0:T(1,128)}) custom-call(bf16[256,512]{1,0:T(8,128)(2,1)} %get-tuple-element.15.refs_0_, bf16[256,512]{1,0:T(8,128)(2,1)} %get-tuple-element.16.refs_1_, f32[3,256,512]{2,1,0:T(8,128)} %get-tuple-element.17.refs_2_, ...), custom_call_target="tpu_custom_call" | custom-call | tf_op jit(solution)/shard_map/pallas_call | solution.py:511
